TPU v7x, 32 devices: a whole 2x2x4 slice. The times are simulated.
32 devices in a mesh: seq: 8 (over y, x, core), head: 4 (over z).
Axes of the slice: x: 2, y: 2, z: 4, core: 2. Of those that a mesh axis runs over, the one named last changes fastest.
Arguments:
- queries: bfloat16 [512, 8192], P('seq', 'head'), may hold values from -6 to 6
- keys: bfloat16 [512, 1024], P('seq'), may hold values from -6 to 6
- values: bfloat16 [512, 1024], P('seq'), may hold values from -6 to 6
- vertical: int32 [64, 8], replicated, may hold values from -1 to 7, as said below
- slash: int32 [64, 8], replicated, may hold values from -1 to 7, as said below
- plan: int32 [64], replicated, may hold values from 0 to 63, each once
Outputs:
- attended: bfloat16 [512, 8192], P('seq', 'head')
Inputs may be any that keep to these rules, and one draw needn't show every extreme that they name: `vertical`: entries of 0 or more name key blocks of 64 positions; -1 marks an unused entry, and every row has at least one used entry. `slash`: entries of 0 or more are offsets back from a query's own block; -1 marks an unused entry; the first entry of every row is 0. `plan`: A permutation of the query heads.
All inputs are finite; a program needn't handle non-finite values.
Results may differ from a plain program's by a relative error of at most 0.0044.
Values may be sent and summed in bfloat16 or wider, within the bound.
No kernel may reach another device: no remote copies, remote signals or barrier semaphores. Data moves between devices by JAX's collectives and lax.ppermute only.
A program may use at most 64 MiB of HBM per device.

v0:
```python
import functools
import math

import jax
import jax.numpy as jnp
from jax import lax
from jax.experimental import pallas as pl
from jax.experimental.pallas import tpu as pltpu
from jax.sharding import PartitionSpec as P

HD = 128
QH = 64
KVH = 8
BLK = 64
GROUP = QH // KVH
HEADS_AT_ONCE = 4
LANES = 128

floor_value = -1e30

SMEM = pl.BlockSpec(memory_space=pltpu.SMEM)
VMEM = pl.BlockSpec(memory_space=pltpu.VMEM)
ANY = pl.BlockSpec(memory_space=pl.ANY)
SMALL = 1024 * 1024


def shift_of(size):
    assert size & (size - 1) == 0
    return size.bit_length() - 1


def entry_bits(table):
    bits = jnp.zeros((1, table.shape[1]), jnp.int32)
    for entry in range(table.shape[0]):
        named = table[entry : entry + 1, :]
        bits = bits | jnp.where(named >= 0, jnp.int32(1) << jnp.maximum(named, 0), 0)
    return bits


class Tally:
    def __init__(self, sources, most):
        self.width = shift_of(most) + 1
        self.per_word = 31 // self.width
        self.words = [jnp.int32(0)] * -(-sources // self.per_word)

    def rank_and_count(self, source):
        if len(self.words) == 1:
            at = source * self.width
            rank = self.words[0] >> at
            self.words[0] = self.words[0] + (jnp.int32(1) << at)
        else:
            word = source // self.per_word
            at = (source - word * self.per_word) * self.width
            held_word = self.words[0]
            for index in range(1, len(self.words)):
                held_word = jnp.where(word == index, self.words[index], held_word)
            rank = held_word >> at
            one = jnp.int32(1) << at
            self.words = [w + jnp.where(word == index, one, 0) for index, w in enumerate(self.words)]
        return rank & ((1 << self.width) - 1)


def route_kernel(half, held, plan, vertical, slash, send, slots, bits):
    own = lax.axis_index("head")
    lead = own & half
    for i in range(2 * held):
        send[i] = half * held
    for distance in range(half):
        slots[half * held + distance] = 0
    for target in range(half):
        tally = Tally(half, held)
        for t in range(held):
            head = plan[(lead + target) * held + t]
            owner = head >> shift_of(held)
            source = owner & (half - 1)
            rank = tally.rank_and_count(source)
            place = ((source ^ target) << shift_of(held)) + rank
            candidate = (head & (held - 1)) + jnp.where(owner == own, 0, held)
            send[jnp.where(source == own - lead, candidate, 2 * held)] = place
    tally = Tally(half, held)
    for t in range(held):
        source = (plan[own * held + t] >> shift_of(held)) & (half - 1)
        rank = tally.rank_and_count(source)
        distance = source ^ (own - lead)
        slots[(distance << shift_of(held)) + rank] = t
        slots[half * held + distance] = rank + 1
    bits[0:1, :] = entry_bits(vertical)
    bits[1:2, :] = entry_bits(slash)


def attention_kernel(seq_size, half, held, kv_heads, send, bits, kv_own, kv_other, near, far, out_ref):
    query_len = near.shape[0]
    key_len = query_len
    own_seq = lax.axis_index("seq")
    own_head = lax.axis_index("head")
    chips = seq_size // 2
    chip_rows = chips * key_len

    piece = lax.broadcasted_iota(jnp.int32, (1, 2 * chip_rows), 1) // key_len
    core = jnp.where(piece < chips, own_seq & 1, 1 - (own_seq & 1))
    block = ((own_seq >> 1) ^ (piece & (chips - 1))) * 2 + core
    back = own_seq - block
    present = back >= 0
    back_shift = jnp.maximum(back, 0)
    row = lax.broadcasted_iota(jnp.int32, (query_len, LANES), 0)
    column = lax.broadcasted_iota(jnp.int32, (query_len, LANES), 1)
    causal = (column <= row) | (column >= key_len)
    score_scale = HD ** (-0.5) * math.log2(math.e)
    per_kv = held // kv_heads

    def rows_of(at):
        return jnp.concatenate([kv_own[:, at : at + HD], kv_other[:, at : at + HD]], axis=0)

    def scores_of(candidates):
        key = rows_of(candidates[0] // per_kv * HD)
        query = jnp.concatenate(
            [(near if i < held else far)[:, i % held * HD : (i % held + 1) * HD] for i in candidates], axis=0
        )
        return lax.dot_general(
            query, key, (((1,), (1,)), ((), ())), preferred_element_type=jnp.float32
        )

    together = min(HEADS_AT_ONCE, per_kv)
    groups = [range(lead, lead + together) for lead in range(0, 2 * held, together)]
    following = scores_of(groups[0])
    for index, candidates in enumerate(groups):
        scores = following
        if index + 1 < len(groups):
            following = scores_of(groups[index + 1])
        value = rows_of((candidates[0] // per_kv + 2 * kv_heads) * HD)
        weights = []
        totals = []
        for at, i in enumerate(candidates):
            head = (own_head if i < held else own_head ^ half) * held + i % held
            hit = ((bits[0, head] >> block) | (bits[1, head] >> back_shift)) & 1
            bias = jnp.where((hit == 1) & present, 0.0, floor_value)
            masked = scores[at * query_len : (at + 1) * query_len] + bias
            masked = jnp.concatenate(
                [jnp.where(causal, masked[:, :LANES], floor_value), masked[:, LANES:]], axis=1
            )
            row_max = jnp.max(masked, axis=1, keepdims=True)
            weight = jnp.exp2((masked - row_max) * score_scale)
            totals.append(1.0 / jnp.sum(weight, axis=1, keepdims=True))
            weights.append(weight.astype(jnp.bfloat16))
        mixture = jnp.dot(
            jnp.concatenate(weights, axis=0), value, preferred_element_type=jnp.float32
        )
        for at, i in enumerate(candidates):
            mix = mixture[at * query_len : (at + 1) * query_len]
            out_ref[send[i]] = (mix * totals[at]).astype(out_ref.dtype)


def place_kernel(half, held, slots, *refs):
    out_ref, done = refs[-2:]
    for distance, ref in enumerate(refs[:-2]):
        arriving = slots[half * held + distance]
        for rank in range(held):

            @pl.when(rank < arriving)
            def _(ref=ref, rank=rank, distance=distance):
                at = pl.multiple_of(slots[distance * held + rank] * HD, HD)
                pltpu.make_async_copy(ref.at[rank], out_ref.at[:, pl.ds(at, HD)], done).start()

    pltpu.make_async_copy(out_ref, out_ref, done).wait()


def per_device(queries, keys, values, vertical, slash, plan):
    seq_size = lax.axis_size("seq")
    head_size = lax.axis_size("head")
    half = head_size // 2
    query_len = queries.shape[0]
    held = queries.shape[1] // HD
    kv_heads = max(1, held // GROUP)
    chips = seq_size // 2
    assert query_len == BLK and plan.shape[0] == held * head_size and chips & (chips - 1) == 0

    far_queries = lax.ppermute(queries, "head", [(i, i ^ half) for i in range(head_size)])

    send, slots, bits = pl.pallas_call(
        functools.partial(route_kernel, half, held),
        out_shape=[
            jax.ShapeDtypeStruct((2 * held + 1,), jnp.int32),
            jax.ShapeDtypeStruct((half * held + half,), jnp.int32),
            jax.ShapeDtypeStruct((2, vertical.shape[0]), jnp.int32),
        ],
        in_specs=[SMEM, VMEM, VMEM],
        out_specs=[SMEM] * 2 + [VMEM],
        compiler_params=pltpu.CompilerParams(vmem_limit_bytes=SMALL),
        name="route",
    )(plan, vertical.T, slash.T)

    own_head = lax.axis_index("head")
    kv = jnp.concatenate(
        [
            lax.dynamic_slice_in_dim(rows, holder * held // GROUP * HD, kv_heads * HD, axis=1)
            for rows in (keys, values)
            for holder in (own_head, own_head ^ half)
        ],
        axis=1,
    )
    pieces = [kv]
    for m in range(1, chips):
        pieces.append(lax.ppermute(kv, "seq", [(i, i ^ (2 * m)) for i in range(seq_size)]))
    pieces, far_queries, send, slots, bits = lax.optimization_barrier(
        (pieces, far_queries, send, slots, bits)
    )
    kv_own = jnp.concatenate(pieces, axis=0)
    kv_other = lax.ppermute(kv_own, "seq", [(i, i ^ 1) for i in range(seq_size)])

    packed = pl.pallas_call(
        functools.partial(attention_kernel, seq_size, half, held, kv_heads),
        out_shape=jax.ShapeDtypeStruct((half * held + 1, query_len, HD), jnp.bfloat16),
        in_specs=[SMEM] * 2 + [VMEM] * 4,
        out_specs=VMEM,
        compiler_params=pltpu.CompilerParams(vmem_limit_bytes=40 * 1024 * 1024),
        name="attention",
    )(send, bits, kv_own, kv_other, queries, far_queries)

    arrived = [
        lax.ppermute(packed[m * held : (m + 1) * held], "head", [(i, i ^ m) for i in range(head_size)])
        for m in range(1, half)
    ]
    return pl.pallas_call(
        functools.partial(place_kernel, half, held),
        out_shape=pltpu.HBM((query_len, held * HD), packed.dtype),
        in_specs=[SMEM] + [ANY] * half,
        out_specs=pl.BlockSpec(memory_space=pltpu.HBM),
        scratch_shapes=[pltpu.SemaphoreType.DMA],
        compiler_params=pltpu.CompilerParams(vmem_limit_bytes=SMALL),
        name="place",
    )(slots, packed, *arrived)


def solution(mesh):
    in_specs = (P("seq", "head"), P("seq", None), P("seq", None), P(), P(), P())
    out_specs = P("seq", "head")
    return jax.shard_map(
        per_device, mesh=mesh, in_specs=in_specs, out_specs=out_specs, check_vma=False
    )
```

profile of v0, /device:TPU:0, one launch (start us, length us, event | category | flops | bytes accessed | tf_op | source)
XLA Modules:
  0.0 30.4 jit_solution(17983465871329229826)
XLA Ops:
  0.0 4.0 %collective-permute-start.3 = (bf16[64,2048]{1,0:T(8,128)(2,1)}, bf16[64,2048]{1,0:T(8,128)(2,1)S(1)}, u32[]{:S(2)}, u32[]{:S(2)}) collective-permute-start(bf16[64,2048]{1,0:T(8,128)(2,1)} %near.1), channel_id=1, source_target_pairs={{0,2},{1,3},{2,0},{3,1},{4,6},{5,7},{6,4},{7,5},{8,10},{9,11},{10,... | collective-permute-start | bytes 786440 | tf_op jit(solution)/shard_map/ppermute | solution.py:177
  4.0 0.8 %constant_dynamic-slice_fusion.1 = (bf16[64,256]{1,0:T(8,128)(2,1)S(1)}, bf16[64,256]{1,0:T(8,128)(2,1)S(1)}, bf16[64,256]{1,0:T(8,128)(2,1)S(1)}, bf16[64,256]{1,0:T(8,128)(2,1)S(1)}) fusion(bf16[64,1024]{1,0:T(8,128)(2,1)} %param.8, s32[]{:T(128)S(6)} %select_n.19, s32[]{:T(128)S(6)} %select_n.21, bf16[64,1024]{1,0:T(8,128)(2,1)} %param.7), kind=kLoop, calls=%fused_computation.6 | loop fusion | bytes 262152 | tf_op jit(solution)/shard_map/dynamic_slice | solution.py:195
  4.9 0.0 copy-start.1
  4.9 0.0 copy-start.2
  4.9 2.5 %collective-permute-start.2 = (bf16[64,1024]{1,0:T(8,128)(2,1)S(1)}, bf16[64,1024]{1,0:T(8,128)(2,1)S(1)}, u32[]{:S(2)}, u32[]{:S(2)}) collective-permute-start(bf16[64,1024]{1,0:T(8,128)(2,1)S(1)} %pad_maximum_fusion), channel_id=1, source_target_pairs={{0,24},{4,28},{8,16},{12,20},{16,8},{20,12},{24,0},{28,4},{1,25},{... | collective-permute-start | bytes 393224 | tf_op jit(solution)/shard_map/ppermute | solution.py:203
  7.4 0.5 %collective-permute-start.1 = (bf16[64,1024]{1,0:T(8,128)(2,1)S(1)}, bf16[64,1024]{1,0:T(8,128)(2,1)S(1)}, u32[]{:S(2)}, u32[]{:S(2)}) collective-permute-start(bf16[64,1024]{1,0:T(8,128)(2,1)S(1)} %pad_maximum_fusion), channel_id=1, source_target_pairs={{0,16},{4,20},{8,24},{12,28},{16,0},{20,4},{24,8},{28,12},{1,17},{... | collective-permute-start | bytes 393224 | tf_op jit(solution)/shard_map/ppermute | solution.py:203
  7.9 0.5 %collective-permute-start = (bf16[64,1024]{1,0:T(8,128)(2,1)S(1)}, bf16[64,1024]{1,0:T(8,128)(2,1)S(1)}, u32[]{:S(2)}, u32[]{:S(2)}) collective-permute-start(bf16[64,1024]{1,0:T(8,128)(2,1)S(1)} %pad_maximum_fusion), channel_id=1, source_target_pairs={{0,8},{4,12},{8,0},{12,4},{16,24},{20,28},{24,16},{28,20},{1,9},{5... | collective-permute-start | bytes 393224 | tf_op jit(solution)/shard_map/ppermute | solution.py:203
  8.5 0.0 copy-start.3
  8.5 0.0 copy-done.1
  8.5 0.0 copy-done.2
  8.5 0.6 %copy-done.3 = s32[64]{0:T(128)S(1)} copy-done((s32[64]{0:T(128)S(1)}, s32[64]{0:T(128)}, u32[]{:S(2)}) %copy-start.3) | copy-done | bytes 280
  9.1 1.4 %route.1 = (s32[33]{0:T(128)S(1)}, s32[34]{0:T(128)S(1)}, s32[2,64]{1,0:T(2,128)S(1)}) custom-call(s32[64]{0:T(128)S(1)} %copy-done.3, s32[8,64]{1,0:T(8,128)S(1)} %bitcast.2, s32[8,64]{1,0:T(8,128)S(1)} %bitcast.3), custom_call_target="tpu_custom_call" | custom-call | tf_op jit(solution)/shard_map/route/pallas_call | solution.py:179
  10.5 0.8 %collective-permute-done.2 = bf16[64,1024]{1,0:T(8,128)(2,1)S(1)} collective-permute-done((bf16[64,1024]{1,0:T(8,128)(2,1)S(1)}, bf16[64,1024]{1,0:T(8,128)(2,1)S(1)}, u32[]{:S(2)}, u32[]{:S(2)}) %collective-permute-start.2) | collective-permute-done | bytes 131104 | tf_op jit(solution)/shard_map/ppermute | solution.py:203
  11.4 2.3 %collective-permute-done.1 = bf16[64,1024]{1,0:T(8,128)(2,1)S(1)} collective-permute-done((bf16[64,1024]{1,0:T(8,128)(2,1)S(1)}, bf16[64,1024]{1,0:T(8,128)(2,1)S(1)}, u32[]{:S(2)}, u32[]{:S(2)}) %collective-permute-start.1) | collective-permute-done | bytes 131104 | tf_op jit(solution)/shard_map/ppermute | solution.py:203
  13.6 0.1 collective-permute-done
  13.7 2.5 %collective-permute-done.3.far = bf16[64,2048]{1,0:T(8,128)(2,1)S(1)} collective-permute-done((bf16[64,2048]{1,0:T(8,128)(2,1)}, bf16[64,2048]{1,0:T(8,128)(2,1)S(1)}, u32[]{:S(2)}, u32[]{:S(2)}) %collective-permute-start.3) | collective-permute-done | bytes 262176 | tf_op jit(solution)/shard_map/ppermute | solution.py:177
  16.2 0.0 copy-start
  16.3 0.1 collective-permute-start.4
  16.3 1.9 %collective-permute-done.4.kv_other = bf16[256,1024]{1,0:T(8,128)(2,1)S(1)} collective-permute-done((bf16[256,1024]{1,0:T(8,128)(2,1)S(1)}, bf16[256,1024]{1,0:T(8,128)(2,1)S(1)}, u32[]{:S(2)}, u32[]{:S(2)}) %collective-permute-start.4) | collective-permute-done | bytes 524320 | tf_op jit(solution)/shard_map/ppermute | solution.py:208
  18.2 0.0 copy-done
  18.2 2.5 %attention.1.refs_0_ = bf16[33,64,128]{2,1,0:T(8,128)(2,1)S(1)} custom-call(s32[33]{0:T(128)S(1)} %get-tuple-element.20.send, s32[2,64]{1,0:T(2,128)S(1)} %get-tuple-element.21.bits, bf16[256,1024]{1,0:T(8,128)(2,1)S(1)} %constant_dynamic-update-slice_fusion.kv_own, bf16[256,1024]{1,0:T(8,128)(2,1)S(1)} %collective-permute-done.4.kv_other, ...), custom_call_target="tpu_custom_call" | custom-call | tf_op jit(solution)/shard_map/attention/pallas_call | solution.py:210
  20.8 0.9 %collective-permute-start.5 = (bf16[16,64,128]{2,1,0:T(8,128)(2,1)S(1)}, bf16[16,64,128]{2,1,0:T(8,128)(2,1)S(1)}, u32[]{:S(2)}, u32[]{:S(2)}) collective-permute-start(bf16[16,64,128]{2,1,0:T(8,128)(2,1)S(1)} %slice.4), channel_id=1, source_target_pairs={{0,1},{1,0},{2,3},{3,2},{4,5},{5,4},{6,7},{7,6},{8,9},{9,8},{10,11... | collective-permute-start | bytes 786440 | tf_op jit(solution)/shard_map/ppermute | solution.py:220
  21.7 7.5 %collective-permute-done.5.refs_1_ = bf16[16,64,128]{2,1,0:T(8,128)(2,1)S(1)} collective-permute-done((bf16[16,64,128]{2,1,0:T(8,128)(2,1)S(1)}, bf16[16,64,128]{2,1,0:T(8,128)(2,1)S(1)}, u32[]{:S(2)}, u32[]{:S(2)}) %collective-permute-start.5) | collective-permute-done | bytes 262176 | tf_op jit(solution)/shard_map/ppermute | solution.py:220
  29.2 1.2 %place.1 = bf16[64,2048]{1,0:T(8,128)(2,1)} custom-call(s32[34]{0:T(128)S(1)} %get-tuple-element.19.slots, bf16[33,64,128]{2,1,0:T(8,128)(2,1)S(1)} %attention.1.refs_0_, bf16[16,64,128]{2,1,0:T(8,128)(2,1)S(1)} %collective-permute-done.5.refs_1_), custom_call_target="tpu_custom_call" | custom-call | tf_op jit(solution)/shard_map/place/pallas_call | solution.py:223
  (6 shorter events, 0.1 us)
Async XLA Ops:
  0.0 16.2 %collective-permute-start.3 = (bf16[64,2048]{1,0:T(8,128)(2,1)}, bf16[64,2048]{1,0:T(8,128)(2,1)S(1)}, u32[]{:S(2)}, u32[]{:S(2)}) collective-permute-start(bf16[64,2048]{1,0:T(8,128)(2,1)} %near.1), channel_id=1, source_target_pairs={{0,2},{1,3},{2,0},{3,1},{4,6},{5,7},{6,4},{7,5},{8,10},{9,11},{10,... | collective-permute-start | bytes 786440 | tf_op jit(solution)/shard_map/ppermute | solution.py:177
  4.9 3.6 %copy-start.1 = (s32[64,8]{0,1:T(8,128)S(1)}, s32[64,8]{0,1:T(8,128)}, u32[]{:S(2)}) copy-start(s32[64,8]{0,1:T(8,128)} %param.9) | copy-start | bytes 6148
  4.9 3.6 %copy-start.2 = (s32[64,8]{0,1:T(8,128)S(1)}, s32[64,8]{0,1:T(8,128)}, u32[]{:S(2)}) copy-start(s32[64,8]{0,1:T(8,128)} %param.10) | copy-start | bytes 6148
  4.9 6.5 %collective-permute-start.2 = (bf16[64,1024]{1,0:T(8,128)(2,1)S(1)}, bf16[64,1024]{1,0:T(8,128)(2,1)S(1)}, u32[]{:S(2)}, u32[]{:S(2)}) collective-permute-start(bf16[64,1024]{1,0:T(8,128)(2,1)S(1)} %pad_maximum_fusion), channel_id=1, source_target_pairs={{0,24},{4,28},{8,16},{12,20},{16,8},{20,12},{24,0},{28,4},{1,25},{... | collective-permute-start | bytes 393224 | tf_op jit(solution)/shard_map/ppermute | solution.py:203
  7.4 6.2 %collective-permute-start.1 = (bf16[64,1024]{1,0:T(8,128)(2,1)S(1)}, bf16[64,1024]{1,0:T(8,128)(2,1)S(1)}, u32[]{:S(2)}, u32[]{:S(2)}) collective-permute-start(bf16[64,1024]{1,0:T(8,128)(2,1)S(1)} %pad_maximum_fusion), channel_id=1, source_target_pairs={{0,16},{4,20},{8,24},{12,28},{16,0},{20,4},{24,8},{28,12},{1,17},{... | collective-permute-start | bytes 393224 | tf_op jit(solution)/shard_map/ppermute | solution.py:203
  7.9 5.8 %collective-permute-start = (bf16[64,1024]{1,0:T(8,128)(2,1)S(1)}, bf16[64,1024]{1,0:T(8,128)(2,1)S(1)}, u32[]{:S(2)}, u32[]{:S(2)}) collective-permute-start(bf16[64,1024]{1,0:T(8,128)(2,1)S(1)} %pad_maximum_fusion), channel_id=1, source_target_pairs={{0,8},{4,12},{8,0},{12,4},{16,24},{20,28},{24,16},{28,20},{1,9},{5... | collective-permute-start | bytes 393224 | tf_op jit(solution)/shard_map/ppermute | solution.py:203
  8.5 0.7 %copy-start.3 = (s32[64]{0:T(128)S(1)}, s32[64]{0:T(128)}, u32[]{:S(2)}) copy-start(s32[64]{0:T(128)} %plan.1) | copy-start | bytes 772
  16.2 2.0 %copy-start = (bf16[64,2048]{1,0:T(8,128)(2,1)S(1)}, bf16[64,2048]{1,0:T(8,128)(2,1)}, u32[]{:S(2)}) copy-start(bf16[64,2048]{1,0:T(8,128)(2,1)} %near.1) | copy-start | bytes 786436
  16.3 2.0 %collective-permute-start.4 = (bf16[256,1024]{1,0:T(8,128)(2,1)S(1)}, bf16[256,1024]{1,0:T(8,128)(2,1)S(1)}, u32[]{:S(2)}, u32[]{:S(2)}) collective-permute-start(bf16[256,1024]{1,0:T(8,128)(2,1)S(1)} %constant_dynamic-update-slice_fusion.kv_own), channel_id=1, source_target_pairs={{0,4},{4,0},{8,12},{12,8},{16,20},{20,16},{24,28},{28,24},{1,5},{5... | collective-permute-start | bytes 1572872 | tf_op jit(solution)/shard_map/ppermute | solution.py:208
  20.8 8.4 %collective-permute-start.5 = (bf16[16,64,128]{2,1,0:T(8,128)(2,1)S(1)}, bf16[16,64,128]{2,1,0:T(8,128)(2,1)S(1)}, u32[]{:S(2)}, u32[]{:S(2)}) collective-permute-start(bf16[16,64,128]{2,1,0:T(8,128)(2,1)S(1)} %slice.4), channel_id=1, source_target_pairs={{0,1},{1,0},{2,3},{3,2},{4,5},{5,4},{6,7},{7,6},{8,9},{9,8},{10,11... | collective-permute-start | bytes 786440 | tf_op jit(solution)/shard_map/ppermute | solution.py:220
where the time goes:
time: 30.6 us; the launch traced here: 30.4 us
  waiting for transfers between devices  15.1 us (49%)
  starting transfers between devices  8.55 us (28%)
  Pallas kernels  5.16 us (17%)
  local copies, waits for them, and re-layouts  1.55 us (5%)
    ppermute x1, waiting for transfers between devices, per_device(): lax.ppermute(packed[m * held:(m + 1) * held], 'head', [(i, i ^ m) for i i...  7.52 us
    ppermute x1, starting transfers between devices, per_device(): lax.ppermute(queries, 'head', [(i, i ^ half) for i in range(head_size)])  4.04 us
    ppermute x3, starting transfers between devices, per_device(): lax.ppermute(kv, 'seq', [(i, i ^ 2 * m) for i in range(seq_size)])  3.55 us
    ppermute x3, waiting for transfers between devices, per_device(): lax.ppermute(kv, 'seq', [(i, i ^ 2 * m) for i in range(seq_size)])  3.17 us
    pallas_call x1, Pallas kernels, per_device(): pl.pallas_call(functools.partial(attention_kernel, seq_size, half, held,...  2.51 us
    ppermute x1, waiting for transfers between devices, per_device(): lax.ppermute(queries, 'head', [(i, i ^ half) for i in range(head_size)])  2.47 us
    ppermute x1, waiting for transfers between devices, per_device(): lax.ppermute(kv_own, 'seq', [(i, i ^ 1) for i in range(seq_size)])  1.9 us
    pallas_call x1, Pallas kernels, per_device(): pl.pallas_call(functools.partial(route_kernel, half, held), out_shape=[ja...  1.41 us
  transfers between devices with their start and end apart: 6, of which 6 were waited for; matrix products, arithmetic and copies ran while one was open for 3% of the time, Pallas kernels for 5%

commit v1 on v0

--- a/solution.py
+++ b/solution.py
@@ -15,6 +15,7 @@
 GROUP = QH // KVH
 HEADS_AT_ONCE = 4
 LANES = 128
+EXCHANGE_PIECES = 4
 
 floor_value = -1e30
 
@@ -88,8 +89,9 @@
     bits[1:2, :] = entry_bits(slash)
 
 
-def attention_kernel(seq_size, half, held, kv_heads, send, bits, kv_own, kv_other, near, far, out_ref):
-    query_len = near.shape[0]
+def attention_kernel(seq_size, half, held, kv_heads, send, bits, kv_own, kv_other, *refs):
+    query_refs, out_ref = refs[:-1], refs[-1]
+    query_len = query_refs[0].shape[0]
     key_len = query_len
     own_seq = lax.axis_index("seq")
     own_head = lax.axis_index("head")
@@ -108,14 +110,14 @@
     score_scale = HD ** (-0.5) * math.log2(math.e)
     per_kv = held // kv_heads
 
+    query_at = [(ref, at) for ref in query_refs for at in range(0, ref.shape[1], HD)]
+
     def rows_of(at):
         return jnp.concatenate([kv_own[:, at : at + HD], kv_other[:, at : at + HD]], axis=0)
 
     def scores_of(candidates):
         key = rows_of(candidates[0] // per_kv * HD)
-        query = jnp.concatenate(
-            [(near if i < held else far)[:, i % held * HD : (i % held + 1) * HD] for i in candidates], axis=0
-        )
+        query = jnp.concatenate([ref[:, at : at + HD] for ref, at in (query_at[i] for i in candidates)], axis=0)
         return lax.dot_general(
             query, key, (((1,), (1,)), ((), ())), preferred_element_type=jnp.float32
         )
@@ -150,16 +152,16 @@
             out_ref[send[i]] = (mix * totals[at]).astype(out_ref.dtype)
 
 
-def place_kernel(half, held, slots, *refs):
+def place_kernel(half, held, chunks, slots, *refs):
     out_ref, done = refs[-2:]
-    for distance, ref in enumerate(refs[:-2]):
+    for (distance, first, count), ref in zip(chunks, refs):
         arriving = slots[half * held + distance]
-        for rank in range(held):
+        for rank in range(first, first + count):
 
             @pl.when(rank < arriving)
-            def _(ref=ref, rank=rank, distance=distance):
+            def _(ref=ref, rank=rank, first=first, distance=distance):
                 at = pl.multiple_of(slots[distance * held + rank] * HD, HD)
-                pltpu.make_async_copy(ref.at[rank], out_ref.at[:, pl.ds(at, HD)], done).start()
+                pltpu.make_async_copy(ref.at[rank - first], out_ref.at[:, pl.ds(at, HD)], done).start()
 
     pltpu.make_async_copy(out_ref, out_ref, done).wait()
 
@@ -173,8 +175,6 @@
     kv_heads = max(1, held // GROUP)
     chips = seq_size // 2
     assert query_len == BLK and plan.shape[0] == held * head_size and chips & (chips - 1) == 0
-
-    far_queries = lax.ppermute(queries, "head", [(i, i ^ half) for i in range(head_size)])
 
     send, slots, bits = pl.pallas_call(
         functools.partial(route_kernel, half, held),
@@ -201,6 +201,11 @@
     pieces = [kv]
     for m in range(1, chips):
         pieces.append(lax.ppermute(kv, "seq", [(i, i ^ (2 * m)) for i in range(seq_size)]))
+    swap = [(i, i ^ half) for i in range(head_size)]
+    cut = held * 10 // 16
+    far_queries = [
+        lax.ppermute(queries[:, first * HD : last * HD], "head", swap) for first, last in ((0, cut), (cut, held))
+    ]
     pieces, far_queries, send, slots, bits = lax.optimization_barrier(
         (pieces, far_queries, send, slots, bits)
     )
@@ -210,20 +215,24 @@
     packed = pl.pallas_call(
         functools.partial(attention_kernel, seq_size, half, held, kv_heads),
         out_shape=jax.ShapeDtypeStruct((half * held + 1, query_len, HD), jnp.bfloat16),
-        in_specs=[SMEM] * 2 + [VMEM] * 4,
+        in_specs=[SMEM] * 2 + [VMEM] * (3 + len(far_queries)),
         out_specs=VMEM,
         compiler_params=pltpu.CompilerParams(vmem_limit_bytes=40 * 1024 * 1024),
         name="attention",
-    )(send, bits, kv_own, kv_other, queries, far_queries)
-
+    )(send, bits, kv_own, kv_other, queries, *far_queries)
+
+    count = max(1, held // EXCHANGE_PIECES)
+    chunks = [(m, first, count) for m in range(1, half) for first in range(0, held, count)]
     arrived = [
-        lax.ppermute(packed[m * held : (m + 1) * held], "head", [(i, i ^ m) for i in range(head_size)])
-        for m in range(1, half)
+        lax.ppermute(
+            packed[m * held + first : m * held + first + count], "head", [(i, i ^ m) for i in range(head_size)]
+        )
+        for m, first, count in chunks
     ]
     return pl.pallas_call(
-        functools.partial(place_kernel, half, held),
+        functools.partial(place_kernel, half, held, [(0, 0, held)] + chunks),
         out_shape=pltpu.HBM((query_len, held * HD), packed.dtype),
-        in_specs=[SMEM] + [ANY] * half,
+        in_specs=[SMEM] + [ANY] * (1 + len(arrived)),
         out_specs=pl.BlockSpec(memory_space=pltpu.HBM),
         scratch_shapes=[pltpu.SemaphoreType.DMA],
         compiler_params=pltpu.CompilerParams(vmem_limit_bytes=SMALL),

time: 30.6 us -> 31.4 us (1.026)
  starting transfers between devices: 8.55 us -> 12 us
  waiting for transfers between devices: 15.1 us -> 12.3 us
    ppermute x2 -> x6, starting transfers between devices: 4.93 us -> 8.38 us  [the longest x2 4.26 us: per_device(): lax.ppermute(queries[:, first * HD:last * HD], 'head', swap)]
    ppermute x3, waiting for transfers between devices: 3.17 us -> 0.01 us  [per_device(): lax.ppermute(kv, 'seq', [(i, i ^ 2 * m) for i in range(seq_size)])]
    slice x1 -> x3, local copies, waits for them, and re-layouts: 0.02 us -> 1 us  [the longest x2 0.98 us: per_device(): queries[:, first * HD:last * HD]]
    dynamic_slice x1, local copies, waits for them, and re-layouts: 0.82 us -> 0.02 us  [per_device(): lax.dynamic_slice_in_dim(rows, holder * held // GROUP * HD, kv_heads * HD...]
    ppermute x2 -> x6, waiting for transfers between devices: 9.99 us -> 10.4 us  [the longest x2 6.07 us: per_device(): lax.ppermute(queries[:, first * HD:last * HD], 'head', swap)]
    unnamed x11 -> x15, local copies, waits for them, and re-layouts: 0.7 us -> 0.7 us
  transfers between devices with their start and end apart: 6 -> 10, of which waited for: 6 -> 6; matrix products, arithmetic and copies ran while one was open for 3% -> 0% of each run, Pallas kernels for 5% -> 4%
where the time goes in v1:
time: 31.4 us; the launch traced here: 31.3 us
  waiting for transfers between devices  12.3 us (39%)
  starting transfers between devices  12 us (38%)
  Pallas kernels  5.14 us (16%)
  local copies, waits for them, and re-layouts  1.73 us (6%)
    ppermute x2, waiting for transfers between devices, per_device(): lax.ppermute(queries[:, first * HD:last * HD], 'head', swap)  6.07 us
    ppermute x4, waiting for transfers between devices, per_device(): lax.ppermute(packed[m * held + first:m * held + first + count], 'head', [...  4.29 us
    ppermute x2, starting transfers between devices, per_device(): lax.ppermute(queries[:, first * HD:last * HD], 'head', swap)  4.26 us
    ppermute x4, starting transfers between devices, per_device(): lax.ppermute(packed[m * held + first:m * held + first + count], 'head', [...  4.12 us
    ppermute x3, starting transfers between devices, per_device(): lax.ppermute(kv, 'seq', [(i, i ^ 2 * m) for i in range(seq_size)])  3.55 us
    pallas_call x1, Pallas kernels, per_device(): pl.pallas_call(functools.partial(attention_kernel, seq_size, half, held,...  2.47 us
    ppermute x1, waiting for transfers between devices, per_device(): lax.ppermute(kv_own, 'seq', [(i, i ^ 1) for i in range(seq_size)])  1.9 us
    pallas_call x1, Pallas kernels, per_device(): pl.pallas_call(functools.partial(route_kernel, half, held), out_shape=[ja...  1.41 us
  transfers between devices with their start and end apart: 10, of which 6 were waited for; matrix products, arithmetic and copies ran while one was open for 0% of the time, Pallas kernels for 4%

profile of v1, /device:TPU:0, one launch (start us, length us, event | category | flops | bytes accessed | tf_op | source)
XLA Modules:
  0.0 31.3 jit_solution(2557790304185514754)
XLA Ops:
  0.0 0.0 copy-start.4
  0.0 0.0 copy-start.5
  0.0 1.0 %slice.18 = bf16[64,1280]{1,0:T(8,128)(2,1)S(1)} slice(bf16[64,2048]{1,0:T(8,128)(2,1)} %refs_0_.1), slice={[0:64], [0:1280]} | slice | bytes 327680 | tf_op jit(solution)/shard_map/slice | solution.py:207
  1.0 4.1 %collective-permute-start.3 = (bf16[64,1280]{1,0:T(8,128)(2,1)S(1)}, bf16[64,1280]{1,0:T(8,128)(2,1)S(1)}, u32[]{:S(2)}, u32[]{:S(2)}) collective-permute-start(bf16[64,1280]{1,0:T(8,128)(2,1)S(1)} %slice.18), channel_id=1, source_target_pairs={{0,2},{1,3},{2,0},{3,1},{4,6},{5,7},{6,4},{7,5},{8,10},{9,11},{10,... | collective-permute-start | bytes 491528 | tf_op jit(solution)/shard_map/ppermute | solution.py:207
  5.1 0.0 copy-done.4
  5.1 0.0 copy-done.5
  5.1 0.0 copy-start
  5.1 2.5 %collective-permute-start.2 = (bf16[64,1024]{1,0:T(8,128)(2,1)S(1)}, bf16[64,1024]{1,0:T(8,128)(2,1)S(1)}, u32[]{:S(2)}, u32[]{:S(2)}) collective-permute-start(bf16[64,1024]{1,0:T(8,128)(2,1)S(1)} %pad_maximum_fusion), channel_id=1, source_target_pairs={{0,24},{4,28},{8,16},{12,20},{16,8},{20,12},{24,0},{28,4},{1,25},{... | collective-permute-start | bytes 393224 | tf_op jit(solution)/shard_map/ppermute | solution.py:203
  7.6 0.5 %collective-permute-start.1 = (bf16[64,1024]{1,0:T(8,128)(2,1)S(1)}, bf16[64,1024]{1,0:T(8,128)(2,1)S(1)}, u32[]{:S(2)}, u32[]{:S(2)}) collective-permute-start(bf16[64,1024]{1,0:T(8,128)(2,1)S(1)} %pad_maximum_fusion), channel_id=1, source_target_pairs={{0,16},{4,20},{8,24},{12,28},{16,0},{20,4},{24,8},{28,12},{1,17},{... | collective-permute-start | bytes 393224 | tf_op jit(solution)/shard_map/ppermute | solution.py:203
  8.1 0.5 %collective-permute-start = (bf16[64,1024]{1,0:T(8,128)(2,1)S(1)}, bf16[64,1024]{1,0:T(8,128)(2,1)S(1)}, u32[]{:S(2)}, u32[]{:S(2)}) collective-permute-start(bf16[64,1024]{1,0:T(8,128)(2,1)S(1)} %pad_maximum_fusion), channel_id=1, source_target_pairs={{0,8},{4,12},{8,0},{12,4},{16,24},{20,28},{24,16},{28,20},{1,9},{5... | collective-permute-start | bytes 393224 | tf_op jit(solution)/shard_map/ppermute | solution.py:203
  8.7 0.0 copy-done
  8.7 0.0 copy-start.1
  8.7 0.0 copy-start.2
  8.7 0.2 collective-permute-start.4
  8.9 0.0 copy-start.3
  8.9 0.5 %copy-done.1 = s32[64,8]{0,1:T(8,128)S(1)} copy-done((s32[64,8]{0,1:T(8,128)S(1)}, s32[64,8]{0,1:T(8,128)}, u32[]{:S(2)}) %copy-start.1) | copy-done | bytes 2072
  9.4 0.0 copy-done.2
  9.4 0.1 copy-done.3
  9.5 1.4 %route.1 = (s32[33]{0:T(128)S(1)}, s32[34]{0:T(128)S(1)}, s32[2,64]{1,0:T(2,128)S(1)}) custom-call(s32[64]{0:T(128)S(1)} %copy-done.3, s32[8,64]{1,0:T(8,128)S(1)} %bitcast.2, s32[8,64]{1,0:T(8,128)S(1)} %bitcast.3), custom_call_target="tpu_custom_call" | custom-call | tf_op jit(solution)/shard_map/route/pallas_call | solution.py:179
  10.9 6.1 %collective-permute-done.4.refs_2_ = bf16[64,768]{1,0:T(8,128)(2,1)S(1)} collective-permute-done((bf16[64,768]{1,0:T(8,128)(2,1)S(1)}, bf16[64,768]{1,0:T(8,128)(2,1)S(1)}, u32[]{:S(2)}, u32[]{:S(2)}) %collective-permute-start.4) | collective-permute-done | bytes 98336 | tf_op jit(solution)/shard_map/ppermute | solution.py:207
  17.0 0.0 collective-permute-done.2
  17.0 0.0 collective-permute-done.1
  17.0 0.0 collective-permute-done
  17.0 0.0 collective-permute-done.3.refs_1_
  17.1 0.1 collective-permute-start.5
  17.2 1.9 %collective-permute-done.5.kv_other = bf16[256,1024]{1,0:T(8,128)(2,1)S(1)} collective-permute-done((bf16[256,1024]{1,0:T(8,128)(2,1)S(1)}, bf16[256,1024]{1,0:T(8,128)(2,1)S(1)}, u32[]{:S(2)}, u32[]{:S(2)}) %collective-permute-start.5) | collective-permute-done | bytes 524320 | tf_op jit(solution)/shard_map/ppermute | solution.py:213
  19.1 2.5 %attention.1.refs_0_ = bf16[33,64,128]{2,1,0:T(8,128)(2,1)S(1)} custom-call(s32[33]{0:T(128)S(1)} %get-tuple-element.21.send, s32[2,64]{1,0:T(2,128)S(1)} %get-tuple-element.22.bits, bf16[256,1024]{1,0:T(8,128)(2,1)S(1)} %constant_dynamic-update-slice_fusion.kv_own, bf16[256,1024]{1,0:T(8,128)(2,1)S(1)} %collective-permute-done.5.kv_other, ...), custom_call_target="tpu_custom_call" | custom-call | tf_op jit(solution)/shard_map/attention/pallas_call | solution.py:215
  21.6 0.8 %collective-permute-start.9 = (bf16[4,64,128]{2,1,0:T(8,128)(2,1)S(1)}, bf16[4,64,128]{2,1,0:T(8,128)(2,1)S(1)}, u32[]{:S(2)}, u32[]{:S(2)}) collective-permute-start(bf16[4,64,128]{2,1,0:T(8,128)(2,1)S(1)} %get-tuple-element.29), channel_id=1, source_target_pairs={{0,1},{1,0},{2,3},{3,2},{4,5},{5,4},{6,7},{7,6},{8,9},{9,8},{10,11... | collective-permute-start | bytes 196616 | tf_op jit(solution)/shard_map/ppermute | solution.py:227
  22.4 1.3 %collective-permute-start.8 = (bf16[4,64,128]{2,1,0:T(8,128)(2,1)S(1)}, bf16[4,64,128]{2,1,0:T(8,128)(2,1)S(1)}, u32[]{:S(2)}, u32[]{:S(2)}) collective-permute-start(bf16[4,64,128]{2,1,0:T(8,128)(2,1)S(1)} %get-tuple-element.30), channel_id=1, source_target_pairs={{0,1},{1,0},{2,3},{3,2},{4,5},{5,4},{6,7},{7,6},{8,9},{9,8},{10,11... | collective-permute-start | bytes 196616 | tf_op jit(solution)/shard_map/ppermute | solution.py:227
  23.7 0.7 %collective-permute-start.7 = (bf16[4,64,128]{2,1,0:T(8,128)(2,1)S(1)}, bf16[4,64,128]{2,1,0:T(8,128)(2,1)S(1)}, u32[]{:S(2)}, u32[]{:S(2)}) collective-permute-start(bf16[4,64,128]{2,1,0:T(8,128)(2,1)S(1)} %get-tuple-element.31), channel_id=1, source_target_pairs={{0,1},{1,0},{2,3},{3,2},{4,5},{5,4},{6,7},{7,6},{8,9},{9,8},{10,11... | collective-permute-start | bytes 196616 | tf_op jit(solution)/shard_map/ppermute | solution.py:227
  24.4 1.3 %collective-permute-start.6 = (bf16[4,64,128]{2,1,0:T(8,128)(2,1)S(1)}, bf16[4,64,128]{2,1,0:T(8,128)(2,1)S(1)}, u32[]{:S(2)}, u32[]{:S(2)}) collective-permute-start(bf16[4,64,128]{2,1,0:T(8,128)(2,1)S(1)} %get-tuple-element.32), channel_id=1, source_target_pairs={{0,1},{1,0},{2,3},{3,2},{4,5},{5,4},{6,7},{7,6},{8,9},{9,8},{10,11... | collective-permute-start | bytes 196616 | tf_op jit(solution)/shard_map/ppermute | solution.py:227
  25.7 0.9 %collective-permute-done.9.refs_4_ = bf16[4,64,128]{2,1,0:T(8,128)(2,1)S(1)} collective-permute-done((bf16[4,64,128]{2,1,0:T(8,128)(2,1)S(1)}, bf16[4,64,128]{2,1,0:T(8,128)(2,1)S(1)}, u32[]{:S(2)}, u32[]{:S(2)}) %collective-permute-start.9) | collective-permute-done | bytes 65568 | tf_op jit(solution)/shard_map/ppermute | solution.py:227
  26.6 1.4 %collective-permute-done.8.refs_3_ = bf16[4,64,128]{2,1,0:T(8,128)(2,1)S(1)} collective-permute-done((bf16[4,64,128]{2,1,0:T(8,128)(2,1)S(1)}, bf16[4,64,128]{2,1,0:T(8,128)(2,1)S(1)}, u32[]{:S(2)}, u32[]{:S(2)}) %collective-permute-start.8) | collective-permute-done | bytes 65568 | tf_op jit(solution)/shard_map/ppermute | solution.py:227
  28.0 1.3 %collective-permute-done.7.refs_2_ = bf16[4,64,128]{2,1,0:T(8,128)(2,1)S(1)} collective-permute-done((bf16[4,64,128]{2,1,0:T(8,128)(2,1)S(1)}, bf16[4,64,128]{2,1,0:T(8,128)(2,1)S(1)}, u32[]{:S(2)}, u32[]{:S(2)}) %collective-permute-start.7) | collective-permute-done | bytes 65568 | tf_op jit(solution)/shard_map/ppermute | solution.py:227
  29.3 0.7 %collective-permute-done.6.refs_1_ = bf16[4,64,128]{2,1,0:T(8,128)(2,1)S(1)} collective-permute-done((bf16[4,64,128]{2,1,0:T(8,128)(2,1)S(1)}, bf16[4,64,128]{2,1,0:T(8,128)(2,1)S(1)}, u32[]{:S(2)}, u32[]{:S(2)}) %collective-permute-start.6) | collective-permute-done | bytes 65568 | tf_op jit(solution)/shard_map/ppermute | solution.py:227
  30.0 1.3 %place.1 = bf16[64,2048]{1,0:T(8,128)(2,1)} custom-call(s32[34]{0:T(128)S(1)} %get-tuple-element.20.slots, bf16[33,64,128]{2,1,0:T(8,128)(2,1)S(1)} %attention.1.refs_0_, bf16[4,64,128]{2,1,0:T(8,128)(2,1)S(1)} %collective-permute-done.6.refs_1_, bf16[4,64,128]{2,1,0:T(8,128)(2,1)S(1)} %collective-permute-done.7.refs_2_, ...), custom_call_target="tpu_custom_call" | custom-call | tf_op jit(solution)/shard_map/place/pallas_call | solution.py:232
  (8 shorter events, 0.1 us)
Async XLA Ops:
  0.0 5.1 %copy-start.4 = (bf16[64,1024]{1,0:T(8,128)(2,1)S(1)}, bf16[64,1024]{1,0:T(8,128)(2,1)}, u32[]{:S(2)}) copy-start(bf16[64,1024]{1,0:T(8,128)(2,1)} %param.8) | copy-start | bytes 393220
  0.0 5.1 %copy-start.5 = (bf16[64,1024]{1,0:T(8,128)(2,1)S(1)}, bf16[64,1024]{1,0:T(8,128)(2,1)}, u32[]{:S(2)}) copy-start(bf16[64,1024]{1,0:T(8,128)(2,1)} %param.7) | copy-start | bytes 393220
  1.0 16.0 %collective-permute-start.3 = (bf16[64,1280]{1,0:T(8,128)(2,1)S(1)}, bf16[64,1280]{1,0:T(8,128)(2,1)S(1)}, u32[]{:S(2)}, u32[]{:S(2)}) collective-permute-start(bf16[64,1280]{1,0:T(8,128)(2,1)S(1)} %slice.18), channel_id=1, source_target_pairs={{0,2},{1,3},{2,0},{3,1},{4,6},{5,7},{6,4},{7,5},{8,10},{9,11},{10,... | collective-permute-start | bytes 491528 | tf_op jit(solution)/shard_map/ppermute | solution.py:207
  5.1 3.6 %copy-start = (bf16[64,2048]{1,0:T(8,128)(2,1)S(1)}, bf16[64,2048]{1,0:T(8,128)(2,1)}, u32[]{:S(2)}) copy-start(bf16[64,2048]{1,0:T(8,128)(2,1)} %refs_0_.1) | copy-start | bytes 786436
  5.1 11.9 %collective-permute-start.2 = (bf16[64,1024]{1,0:T(8,128)(2,1)S(1)}, bf16[64,1024]{1,0:T(8,128)(2,1)S(1)}, u32[]{:S(2)}, u32[]{:S(2)}) collective-permute-start(bf16[64,1024]{1,0:T(8,128)(2,1)S(1)} %pad_maximum_fusion), channel_id=1, source_target_pairs={{0,24},{4,28},{8,16},{12,20},{16,8},{20,12},{24,0},{28,4},{1,25},{... | collective-permute-start | bytes 393224 | tf_op jit(solution)/shard_map/ppermute | solution.py:203
  7.6 9.4 %collective-permute-start.1 = (bf16[64,1024]{1,0:T(8,128)(2,1)S(1)}, bf16[64,1024]{1,0:T(8,128)(2,1)S(1)}, u32[]{:S(2)}, u32[]{:S(2)}) collective-permute-start(bf16[64,1024]{1,0:T(8,128)(2,1)S(1)} %pad_maximum_fusion), channel_id=1, source_target_pairs={{0,16},{4,20},{8,24},{12,28},{16,0},{20,4},{24,8},{28,12},{1,17},{... | collective-permute-start | bytes 393224 | tf_op jit(solution)/shard_map/ppermute | solution.py:203
  8.1 8.9 %collective-permute-start = (bf16[64,1024]{1,0:T(8,128)(2,1)S(1)}, bf16[64,1024]{1,0:T(8,128)(2,1)S(1)}, u32[]{:S(2)}, u32[]{:S(2)}) collective-permute-start(bf16[64,1024]{1,0:T(8,128)(2,1)S(1)} %pad_maximum_fusion), channel_id=1, source_target_pairs={{0,8},{4,12},{8,0},{12,4},{16,24},{20,28},{24,16},{28,20},{1,9},{5... | collective-permute-start | bytes 393224 | tf_op jit(solution)/shard_map/ppermute | solution.py:203
  8.7 0.7 %copy-start.1 = (s32[64,8]{0,1:T(8,128)S(1)}, s32[64,8]{0,1:T(8,128)}, u32[]{:S(2)}) copy-start(s32[64,8]{0,1:T(8,128)} %param.9) | copy-start | bytes 6148
  8.7 0.7 %copy-start.2 = (s32[64,8]{0,1:T(8,128)S(1)}, s32[64,8]{0,1:T(8,128)}, u32[]{:S(2)}) copy-start(s32[64,8]{0,1:T(8,128)} %param.10) | copy-start | bytes 6148
  8.7 8.3 %collective-permute-start.4 = (bf16[64,768]{1,0:T(8,128)(2,1)S(1)}, bf16[64,768]{1,0:T(8,128)(2,1)S(1)}, u32[]{:S(2)}, u32[]{:S(2)}) collective-permute-start(bf16[64,768]{1,0:T(8,128)(2,1)S(1)} %slice.19), channel_id=1, source_target_pairs={{0,2},{1,3},{2,0},{3,1},{4,6},{5,7},{6,4},{7,5},{8,10},{9,11},{10,... | collective-permute-start | bytes 294920 | tf_op jit(solution)/shard_map/ppermute | solution.py:207
  8.9 0.7 %copy-start.3 = (s32[64]{0:T(128)S(1)}, s32[64]{0:T(128)}, u32[]{:S(2)}) copy-start(s32[64]{0:T(128)} %plan.1) | copy-start | bytes 772
  17.1 2.0 %collective-permute-start.5 = (bf16[256,1024]{1,0:T(8,128)(2,1)S(1)}, bf16[256,1024]{1,0:T(8,128)(2,1)S(1)}, u32[]{:S(2)}, u32[]{:S(2)}) collective-permute-start(bf16[256,1024]{1,0:T(8,128)(2,1)S(1)} %constant_dynamic-update-slice_fusion.kv_own), channel_id=1, source_target_pairs={{0,4},{4,0},{8,12},{12,8},{16,20},{20,16},{24,28},{28,24},{1,5},{5... | collective-permute-start | bytes 1572872 | tf_op jit(solution)/shard_map/ppermute | solution.py:213
  21.6 5.0 %collective-permute-start.9 = (bf16[4,64,128]{2,1,0:T(8,128)(2,1)S(1)}, bf16[4,64,128]{2,1,0:T(8,128)(2,1)S(1)}, u32[]{:S(2)}, u32[]{:S(2)}) collective-permute-start(bf16[4,64,128]{2,1,0:T(8,128)(2,1)S(1)} %get-tuple-element.29), channel_id=1, source_target_pairs={{0,1},{1,0},{2,3},{3,2},{4,5},{5,4},{6,7},{7,6},{8,9},{9,8},{10,11... | collective-permute-start | bytes 196616 | tf_op jit(solution)/shard_map/ppermute | solution.py:227
  22.4 5.6 %collective-permute-start.8 = (bf16[4,64,128]{2,1,0:T(8,128)(2,1)S(1)}, bf16[4,64,128]{2,1,0:T(8,128)(2,1)S(1)}, u32[]{:S(2)}, u32[]{:S(2)}) collective-permute-start(bf16[4,64,128]{2,1,0:T(8,128)(2,1)S(1)} %get-tuple-element.30), channel_id=1, source_target_pairs={{0,1},{1,0},{2,3},{3,2},{4,5},{5,4},{6,7},{7,6},{8,9},{9,8},{10,11... | collective-permute-start | bytes 196616 | tf_op jit(solution)/shard_map/ppermute | solution.py:227
  23.7 5.6 %collective-permute-start.7 = (bf16[4,64,128]{2,1,0:T(8,128)(2,1)S(1)}, bf16[4,64,128]{2,1,0:T(8,128)(2,1)S(1)}, u32[]{:S(2)}, u32[]{:S(2)}) collective-permute-start(bf16[4,64,128]{2,1,0:T(8,128)(2,1)S(1)} %get-tuple-element.31), channel_id=1, source_target_pairs={{0,1},{1,0},{2,3},{3,2},{4,5},{5,4},{6,7},{7,6},{8,9},{9,8},{10,11... | collective-permute-start | bytes 196616 | tf_op jit(solution)/shard_map/ppermute | solution.py:227
  24.4 5.6 %collective-permute-start.6 = (bf16[4,64,128]{2,1,0:T(8,128)(2,1)S(1)}, bf16[4,64,128]{2,1,0:T(8,128)(2,1)S(1)}, u32[]{:S(2)}, u32[]{:S(2)}) collective-permute-start(bf16[4,64,128]{2,1,0:T(8,128)(2,1)S(1)} %get-tuple-element.32), channel_id=1, source_target_pairs={{0,1},{1,0},{2,3},{3,2},{4,5},{5,4},{6,7},{7,6},{8,9},{9,8},{10,11... | collective-permute-start | bytes 196616 | tf_op jit(solution)/shard_map/ppermute | solution.py:227
